TPU v7x, 128 devices: a whole 4x4x4 slice. The times are simulated.
128 devices in a mesh: radial: 16 (over x, y), col: 8 (over z, core).
Axes of the slice: x: 4, y: 4, z: 4, core: 2. Of those that a mesh axis runs over, the one named last changes fastest.
Arguments:
- forcing: bfloat16 [4, 32, 2, 128, 1024], P(None, 'radial', None, None, 'col'), may hold values from -6 to 6
- inverses: bfloat16 [4, 32, 2, 1024, 1024], P(None, 'radial', None, None, 'col'), may hold values from -0.125 to 0.125
- couplings: bfloat16 [4, 32, 2, 2, 1024, 1024], P(None, 'radial', None, None, None, 'col'), may hold values from -0.09375 to 0.09375
Outputs:
- solution: float32 [4, 32, 2, 128, 1024], P(None, 'radial', None, None, 'col')
All inputs are finite; a program needn't handle non-finite values.
Results may differ from a plain program's by a relative error of at most 0.0085.
Values may be sent and summed in bfloat16 or wider, within the bound.
A program may use at most 128 MiB of HBM per device.

v0:
```python
import jax
import jax.numpy as jnp
from jax import lax
from jax.sharding import PartitionSpec as P


def from_behind(value, axis, steps):
    count = lax.axis_size(axis)
    leading, last = (max(0, -steps), min(count, count - steps))
    return lax.ppermute(value, axis, [(source, source + steps) for source in range(leading, last)])


def conj_product(gathered, factor):
    real_part = jnp.einsum(
        "frk,fkn->frn", gathered[:, 0], factor[:, 0], preferred_element_type=jnp.float32
    )
    real_part = real_part + jnp.einsum(
        "frk,fkn->frn", gathered[:, 1], factor[:, 1], preferred_element_type=jnp.float32
    )
    imag_part = jnp.einsum(
        "frk,fkn->frn", gathered[:, 1], factor[:, 0], preferred_element_type=jnp.float32
    )
    imag_part = imag_part - jnp.einsum(
        "frk,fkn->frn", gathered[:, 0], factor[:, 1], preferred_element_type=jnp.float32
    )
    return jnp.stack([real_part, imag_part], axis=1)


def zero_panel(gathered, factor):
    return jnp.zeros((gathered.shape[0], 2, gathered.shape[2], factor.shape[-1]), jnp.float32)


def back_step(gathered, from_lower, inverse, coupling_low):
    return conj_product(gathered, inverse) - conj_product(from_lower, coupling_low)


def back_none(gathered, from_lower, inverse, coupling_low):
    return zero_panel(gathered, inverse)


def gather_rhs(panel_shard):
    return lax.all_gather(panel_shard.astype(jnp.bfloat16), "col", axis=3, tiled=True)


def bring_lower(panel_shard, distance):
    pieces = panel_shard.astype(jnp.bfloat16)
    gathered = lax.all_gather(pieces, "col", axis=3, tiled=True)
    from_lower = from_behind(gathered, "radial", distance)
    return from_lower


def local(forcing, inverses, couplings):
    local_rows = forcing.shape[1]
    all_rows = local_rows * lax.axis_size("radial")
    levels = all_rows.bit_length() - 1
    position = lax.axis_index("radial")
    panels = [forcing[:, member].astype(jnp.float32) for member in range(local_rows)]
    nothing = jnp.zeros_like(panels[0])
    plan = []
    for depth_level in range(levels):
        stride = 2**depth_level
        if stride < local_rows:
            members = [member for member in range(local_rows) if member % (2 * stride) == stride]
            plan.append((stride, members, None))
        else:
            plan.append((stride, [0], position * local_rows % (2 * stride) == stride))
    stored = {}
    for stride, members, active in plan:
        for member in members:
            gathered = gather_rhs(panels[member])
            if active is None:
                stored[member] = gathered
            else:
                stored[member] = jnp.where(
                    active, gathered, stored.get(member, jnp.zeros_like(gathered))
                )
            toward_low = couplings[:, member, 0]
            if active is None:
                panels[member - stride] = panels[member - stride] - conj_product(
                    gathered, toward_low
                )
            else:
                to_left = lax.cond(active, conj_product, zero_panel, gathered, toward_low)
                distance = stride // local_rows
                arrived = from_behind(to_left, "radial", -distance)
                panels[0] = panels[0] - arrived
    solved = [nothing for member in range(local_rows)]
    at_top = position == 0
    head_panel = gather_rhs(panels[0])
    solved[0] = lax.cond(at_top, conj_product, zero_panel, head_panel, inverses[:, 0])
    for stride, members, active in reversed(plan):
        for member in members:
            gathered = stored[member]
            if active is None:
                from_lower = lax.all_gather(
                    solved[member - stride].astype(jnp.bfloat16), "col", axis=3, tiled=True
                )
                solved[member] = back_step(
                    gathered, from_lower, inverses[:, member], couplings[:, member, 1]
                )
            else:
                from_lower = bring_lower(solved[0], stride // local_rows)
                result = lax.cond(
                    active,
                    back_step,
                    back_none,
                    gathered,
                    from_lower,
                    inverses[:, member],
                    couplings[:, member, 1],
                )
                solved[member] = jnp.where(active, result, solved[member])
    return jnp.stack(solved, axis=1)


def solution(mesh):
    return jax.shard_map(
        local,
        mesh=mesh,
        in_specs=(
            P(None, "radial", None, None, "col"),
            P(None, "radial", None, None, "col"),
            P(None, "radial", None, None, None, "col"),
        ),
        out_specs=P(None, "radial", None, None, "col"),
        check_vma=False,
    )
```

profile of v0, /device:TPU:27, one launch (start us, length us, event | category | flops | bytes accessed | tf_op | source)
XLA Modules:
  0.0 676.4 jit_solution(14016527634118119551)
XLA Ops:
  6.5 1.1 fusion.286
  8.4 5.2 fusion.284
  13.6 1.5 copy.42
  15.1 24.0 %all-gather.33.cloned.1.call-done = bf16[4,1,2,128,1024]{4,3,0,2,1:T(8,128)(2,1)} async-done(((bf16[4,1,2,128,128]{4,3,0,2,1:T(8,128)(2,1)}), bf16[4,1,2,128,1024]{4,3,0,2,1:T(8,128)(2,1)}) %all-gather.33.cloned.1.call-update) | async-done | bytes 2097168 | tf_op jit(solution)/shard_map/all_gather | solution.py:42
  39.0 2.1 fusion.266
  41.3 1.8 fusion.267
  44.9 1.5 copy.41
  46.3 26.9 %all-gather.13.cloned.1.call-done = bf16[4,2,128,1024]{3,2,0,1:T(8,128)(2,1)} async-done(((bf16[4,2,128,128]{3,2,0,1:T(8,128)(2,1)}), bf16[4,2,128,1024]{3,2,0,1:T(8,128)(2,1)}) %all-gather.13.cloned.1.call-update) | async-done | bytes 2097168 | tf_op jit(solution)/shard_map/all_gather | solution.py:42
  73.3 5.0 conditional.9
  73.3 2.1 fusion.4
  75.5 1.8 fusion
  78.3 1.9 collective-permute-start
  80.2 15.3 %collective-permute-done = f32[4,2,128,128]{3,2,0,1:T(8,128)S(1)} collective-permute-done((f32[4,2,128,128]{3,2,0,1:T(8,128)S(1)}, f32[4,2,128,128]{3,2,0,1:T(8,128)S(1)}, u32[]{:S(2)}, u32[]{:S(2)}) %collective-permute-start) | collective-permute-done | bytes 524320 | tf_op jit(solution)/shard_map/ppermute | solution.py:10
  95.6 0.8 fusion.278
  96.4 28.9 %all-gather.15.cloned.1.call-done = bf16[4,2,128,1024]{3,2,0,1:T(8,128)(2,1)} async-done(((bf16[4,2,128,128]{3,2,0,1:T(8,128)(2,1)}), bf16[4,2,128,1024]{3,2,0,1:T(8,128)(2,1)}) %all-gather.15.cloned.1.call-update) | async-done | bytes 2097168 | tf_op jit(solution)/shard_map/all_gather | solution.py:42
  125.4 3.0 collective-permute-start.1
  128.5 14.5 %collective-permute-done.1 = f32[4,2,128,128]{3,2,0,1:T(8,128)S(1)} collective-permute-done((f32[4,2,128,128]{3,2,0,1:T(8,128)S(1)}, f32[4,2,128,128]{3,2,0,1:T(8,128)S(1)}, u32[]{:S(2)}, u32[]{:S(2)}) %collective-permute-start.1) | collective-permute-done | bytes 524320 | tf_op jit(solution)/shard_map/ppermute | solution.py:10
  143.0 0.8 fusion.282
  143.9 34.2 %all-gather.17.cloned.1.call-done = bf16[4,2,128,1024]{3,2,0,1:T(8,128)(2,1)} async-done(((bf16[4,2,128,128]{3,2,0,1:T(8,128)(2,1)}), bf16[4,2,128,1024]{3,2,0,1:T(8,128)(2,1)}) %all-gather.17.cloned.1.call-update) | async-done | bytes 2097168 | tf_op jit(solution)/shard_map/all_gather | solution.py:42
  178.1 2.3 collective-permute-start.2
  180.4 13.0 %collective-permute-done.2 = f32[4,2,128,128]{3,2,0,1:T(8,128)S(1)} collective-permute-done((f32[4,2,128,128]{3,2,0,1:T(8,128)S(1)}, f32[4,2,128,128]{3,2,0,1:T(8,128)S(1)}, u32[]{:S(2)}, u32[]{:S(2)}) %collective-permute-start.2) | collective-permute-done | bytes 524320 | tf_op jit(solution)/shard_map/ppermute | solution.py:10
  193.4 0.8 fusion.281
  194.3 30.6 %all-gather.19.cloned.1.call-done = bf16[4,2,128,1024]{3,2,0,1:T(8,128)(2,1)} async-done(((bf16[4,2,128,128]{3,2,0,1:T(8,128)(2,1)}), bf16[4,2,128,1024]{3,2,0,1:T(8,128)(2,1)}) %all-gather.19.cloned.1.call-update) | async-done | bytes 2097168 | tf_op jit(solution)/shard_map/all_gather | solution.py:42
  224.9 1.3 collective-permute-start.3
  226.2 15.4 %collective-permute-done.3 = f32[4,2,128,128]{3,2,0,1:T(8,128)S(1)} collective-permute-done((f32[4,2,128,128]{3,2,0,1:T(8,128)S(1)}, f32[4,2,128,128]{3,2,0,1:T(8,128)S(1)}, u32[]{:S(2)}, u32[]{:S(2)}) %collective-permute-start.3) | collective-permute-done | bytes 524320 | tf_op jit(solution)/shard_map/ppermute | solution.py:10
  241.5 0.8 subtract_convert_fusion
  242.4 2.5 fusion.285
  244.9 1.5 copy.40
  246.4 23.7 %all-gather.21.cloned.1.call-done = bf16[4,2,128,1024]{3,2,0,1:T(8,128)(2,1)} async-done(((bf16[4,2,128,128]{3,2,0,1:T(8,128)(2,1)}), bf16[4,2,128,1024]{3,2,0,1:T(8,128)(2,1)}) %all-gather.21.cloned.1.call-update) | async-done | bytes 2097168 | tf_op jit(solution)/shard_map/all_gather | solution.py:42
  271.2 29.0 %all-gather.23.cloned.1.call-done = bf16[4,2,128,1024]{3,2,0,1:T(8,128)(2,1)} async-done(((bf16[4,2,128,128]{3,2,0,1:T(8,128)(2,1)}), bf16[4,2,128,1024]{3,2,0,1:T(8,128)(2,1)}) %all-gather.23.cloned.1.call-update) | async-done | bytes 2097168 | tf_op jit(solution)/shard_map/all_gather | solution.py:47
  300.1 3.8 collective-permute-start.4
  304.0 3.3 copy.39
  307.3 2.0 select_select_fusion
  309.3 39.6 %collective-permute-done.4 = bf16[4,2,128,1024]{3,2,0,1:T(8,128)(2,1)S(1)} collective-permute-done((bf16[4,2,128,1024]{3,2,0,1:T(8,128)(2,1)}, bf16[4,2,128,1024]{3,2,0,1:T(8,128)(2,1)S(1)}, u32[]{:S(2)}, u32[]{:S(2)}) %collective-permute-start.4) | collective-permute-done | bytes 2097184 | tf_op jit(solution)/shard_map/ppermute | solution.py:10
  348.9 0.8 copy-done.17
  349.7 0.8 fusion.280
  350.6 37.6 %all-gather.25.cloned.1.call-done = bf16[4,2,128,1024]{3,2,0,1:T(8,128)(2,1)} async-done(((bf16[4,2,128,128]{3,2,0,1:T(8,128)(2,1)}), bf16[4,2,128,1024]{3,2,0,1:T(8,128)(2,1)}) %all-gather.25.cloned.1.call-update) | async-done | bytes 2097168 | tf_op jit(solution)/shard_map/all_gather | solution.py:47
  388.1 3.1 collective-permute-start.5
  391.2 46.1 %collective-permute-done.5 = bf16[4,2,128,1024]{3,2,0,1:T(8,128)(2,1)} collective-permute-done((bf16[4,2,128,1024]{3,2,0,1:T(8,128)(2,1)}, bf16[4,2,128,1024]{3,2,0,1:T(8,128)(2,1)}, u32[]{:S(2)}, u32[]{:S(2)}) %collective-permute-start.5) | collective-permute-done | bytes 2097184 | tf_op jit(solution)/shard_map/ppermute | solution.py:10
  437.4 0.8 fusion.276
  438.2 39.3 %all-gather.27.cloned.1.call-done = bf16[4,2,128,1024]{3,2,0,1:T(8,128)(2,1)} async-done(((bf16[4,2,128,128]{3,2,0,1:T(8,128)(2,1)}), bf16[4,2,128,1024]{3,2,0,1:T(8,128)(2,1)}) %all-gather.27.cloned.1.call-update) | async-done | bytes 2097168 | tf_op jit(solution)/shard_map/all_gather | solution.py:47
  477.5 3.9 collective-permute-start.6
  481.4 46.7 %collective-permute-done.6 = bf16[4,2,128,1024]{3,2,0,1:T(8,128)(2,1)} collective-permute-done((bf16[4,2,128,1024]{3,2,0,1:T(8,128)(2,1)}, bf16[4,2,128,1024]{3,2,0,1:T(8,128)(2,1)}, u32[]{:S(2)}, u32[]{:S(2)}) %collective-permute-start.6) | collective-permute-done | bytes 2097184 | tf_op jit(solution)/shard_map/ppermute | solution.py:10
  528.4 0.8 copy-done.18
  529.2 1.8 fusion.279
  531.1 41.9 %all-gather.29.cloned.1.call-done = bf16[4,2,128,1024]{3,2,0,1:T(8,128)(2,1)} async-done(((bf16[4,2,128,128]{3,2,0,1:T(8,128)(2,1)}), bf16[4,2,128,1024]{3,2,0,1:T(8,128)(2,1)}) %all-gather.29.cloned.1.call-update) | async-done | bytes 2097168 | tf_op jit(solution)/shard_map/all_gather | solution.py:47
  573.1 3.0 collective-permute-start.7
  576.1 46.1 %collective-permute-done.7 = bf16[4,2,128,1024]{3,2,0,1:T(8,128)(2,1)} collective-permute-done((bf16[4,2,128,1024]{3,2,0,1:T(8,128)(2,1)}, bf16[4,2,128,1024]{3,2,0,1:T(8,128)(2,1)}, u32[]{:S(2)}, u32[]{:S(2)}) %collective-permute-start.7) | collective-permute-done | bytes 2097184 | tf_op jit(solution)/shard_map/ppermute | solution.py:10
  622.2 12.8 %conditional.17 = (f32[4,2,128,128]{3,2,0,1:T(8,128)S(1)}) conditional(s32[]{:T(128)} %convert_element_type.57, () %tuple.59, (bf16[4,2,128,1024]{3,2,0,1:T(8,128)(2,1)}, bf16[4,2,1024,128]{3,2,0,1:T(8,128)(2,1)}, bf16[4,2,128,1024]{3,2,0,1:T(8,128)(2,1)}, bf16[4,2,1024,128]{3,2,0,1:T(8,128)(2,1)}) %tuple.138), branch_computations={%region_16.17_spmd, %region_17.18_spmd} | conditional | flops 1074397184 | bytes 46661724 | solution.py:103
  622.2 2.1 fusion.236
  624.4 1.8 fusion.222
  627.2 1.2 copy-done.14
  628.4 1.6 fusion.226
  630.0 1.6 fusion.220
  631.7 1.6 fusion.230
  633.3 1.6 fusion.221
  635.0 0.8 fusion.274
  636.0 1.4 copy-done
  637.6 1.4 copy-done.31
  640.3 1.1 fusion.263
  641.4 0.8 fusion.275
  642.3 22.5 %all-gather.31.cloned.1.call-done = bf16[4,2,128,1024]{3,2,0,1:T(8,128)(2,1)} async-done(((bf16[4,2,128,128]{3,2,0,1:T(8,128)(2,1)}), bf16[4,2,128,1024]{3,2,0,1:T(8,128)(2,1)}) %all-gather.31.cloned.1.call-update) | async-done | bytes 2097168 | tf_op jit(solution)/shard_map/all_gather | solution.py:95
  664.8 1.8 fusion.271
  668.8 1.1 copy.12
  (88 shorter events, 10.7 us)
Async XLA Ops:
  6.5 32.5 %all-gather.33.cloned.1.call-start = ((), (), s32[]{:S(2)}) async-start(), calls=%async_computation.10 | async-start | bytes 2359296 | tf_op jit(solution)/shard_map/all_gather | solution.py:42
  8.4 64.9 %all-gather.13.cloned.1.call-start = ((), (), s32[]{:S(2)}) async-start(), calls=%async_computation | async-start | bytes 2359296 | tf_op jit(solution)/shard_map/all_gather | solution.py:42
  39.0 2.2 copy-start.15
  41.3 1.9 copy-start.30
  44.8 80.6 %all-gather.15.cloned.1.call-start = ((), (), s32[]{:S(2)}) async-start(), calls=%async_computation.1 | async-start | bytes 2359296 | tf_op jit(solution)/shard_map/all_gather | solution.py:42
  73.3 2.2 copy-start.8
  75.5 1.9 copy-start.20
  78.3 17.3 %collective-permute-start = (f32[4,2,128,128]{3,2,0,1:T(8,128)S(1)}, f32[4,2,128,128]{3,2,0,1:T(8,128)S(1)}, u32[]{:S(2)}, u32[]{:S(2)}) collective-permute-start(f32[4,2,128,128]{3,2,0,1:T(8,128)S(1)} %get-tuple-element.126), channel_id=1, source_target_pairs={{8,0},{16,8},{24,16},{32,24},{40,32},{48,40},{56,48},{64,56},{72,6... | collective-permute-start | bytes 1572872 | tf_op jit(solution)/shard_map/ppermute | solution.py:10
  96.4 81.7 %all-gather.17.cloned.1.call-start = ((), (), s32[]{:S(2)}) async-start(), calls=%async_computation.2 | async-start | bytes 2359296 | tf_op jit(solution)/shard_map/all_gather | solution.py:42
  125.4 17.6 %collective-permute-start.1 = (f32[4,2,128,128]{3,2,0,1:T(8,128)S(1)}, f32[4,2,128,128]{3,2,0,1:T(8,128)S(1)}, u32[]{:S(2)}, u32[]{:S(2)}) collective-permute-start(f32[4,2,128,128]{3,2,0,1:T(8,128)S(1)} %get-tuple-element.127), channel_id=1, source_target_pairs={{16,0},{24,8},{32,16},{40,24},{48,32},{56,40},{64,48},{72,56},{80,... | collective-permute-start | bytes 1572872 | tf_op jit(solution)/shard_map/ppermute | solution.py:10
  143.8 81.0 %all-gather.19.cloned.1.call-start = ((), (), s32[]{:S(2)}) async-start(), calls=%async_computation.3 | async-start | bytes 2359296 | tf_op jit(solution)/shard_map/all_gather | solution.py:42
  178.1 46.7 %copy-start.7 = (bf16[4,1,1,2,1024,128]{5,4,0,3,2,1:T(8,128)(2,1)S(1)}, bf16[4,1,1,2,1024,128]{5,4,0,3,2,1:T(8,128)(2,1)}, u32[]{:S(2)}) copy-start(bf16[4,1,1,2,1024,128]{5,4,0,3,2,1:T(8,128)(2,1)} %copy.41) | copy-start | bytes 6291460
  178.1 15.3 %collective-permute-start.2 = (f32[4,2,128,128]{3,2,0,1:T(8,128)S(1)}, f32[4,2,128,128]{3,2,0,1:T(8,128)S(1)}, u32[]{:S(2)}, u32[]{:S(2)}) collective-permute-start(f32[4,2,128,128]{3,2,0,1:T(8,128)S(1)} %get-tuple-element.128), channel_id=1, source_target_pairs={{32,0},{40,8},{48,16},{56,24},{64,32},{72,40},{80,48},{88,56},{96,... | collective-permute-start | bytes 1572872 | tf_op jit(solution)/shard_map/ppermute | solution.py:10
  194.2 75.9 %all-gather.21.cloned.1.call-start = ((), (), s32[]{:S(2)}) async-start(), calls=%async_computation.4 | async-start | bytes 2359296 | tf_op jit(solution)/shard_map/all_gather | solution.py:42
  224.9 16.7 %collective-permute-start.3 = (f32[4,2,128,128]{3,2,0,1:T(8,128)S(1)}, f32[4,2,128,128]{3,2,0,1:T(8,128)S(1)}, u32[]{:S(2)}, u32[]{:S(2)}) collective-permute-start(f32[4,2,128,128]{3,2,0,1:T(8,128)S(1)} %get-tuple-element.129), channel_id=1, source_target_pairs={{64,0},{72,8},{80,16},{88,24},{96,32},{104,40},{112,48},{120,56},{... | collective-permute-start | bytes 1572872 | tf_op jit(solution)/shard_map/ppermute | solution.py:10
  242.3 57.8 %all-gather.23.cloned.1.call-start = ((), (), s32[]{:S(2)}) async-start(), calls=%async_computation.5 | async-start | bytes 2359296 | tf_op jit(solution)/shard_map/all_gather | solution.py:47
  271.1 117.0 %all-gather.25.cloned.1.call-start = ((), (), s32[]{:S(2)}) async-start(), calls=%async_computation.6 | async-start | bytes 2359296 | tf_op jit(solution)/shard_map/all_gather | solution.py:47
  300.1 48.8 %collective-permute-start.4 = (bf16[4,2,128,1024]{3,2,0,1:T(8,128)(2,1)}, bf16[4,2,128,1024]{3,2,0,1:T(8,128)(2,1)S(1)}, u32[]{:S(2)}, u32[]{:S(2)}) collective-permute-start(bf16[4,2,128,1024]{3,2,0,1:T(8,128)(2,1)} %all-gather.23.cloned.1.call-done), channel_id=1, source_target_pairs={{0,64},{8,72},{16,80},{24,88},{32,96},{40,104},{48,112},{56,120},{... | collective-permute-start | bytes 6291464 | tf_op jit(solution)/shard_map/ppermute | solution.py:10
  303.9 3.3 copy-start.19
  304.0 3.3 copy-start.21
  348.9 0.8 copy-start.17
  350.5 86.9 %copy-start.1 = (f32[4,2,128,128]{3,2,0,1:T(8,128)}, f32[4,2,128,128]{3,2,0,1:T(8,128)S(1)}, u32[]{:S(2)}) copy-start(f32[4,2,128,128]{3,2,0,1:T(8,128)S(1)} %get-tuple-element.113) | copy-start | bytes 1572868
  350.5 126.9 %all-gather.27.cloned.1.call-start = ((), (), s32[]{:S(2)}) async-start(), calls=%async_computation.7 | async-start | bytes 2359296 | tf_op jit(solution)/shard_map/all_gather | solution.py:47
  388.1 49.2 %collective-permute-start.5 = (bf16[4,2,128,1024]{3,2,0,1:T(8,128)(2,1)}, bf16[4,2,128,1024]{3,2,0,1:T(8,128)(2,1)}, u32[]{:S(2)}, u32[]{:S(2)}) collective-permute-start(bf16[4,2,128,1024]{3,2,0,1:T(8,128)(2,1)} %all-gather.25.cloned.1.call-done), channel_id=1, source_target_pairs={{0,32},{8,40},{16,48},{24,56},{32,64},{40,72},{48,80},{56,88},{64,... | collective-permute-start | bytes 6291464 | tf_op jit(solution)/shard_map/ppermute | solution.py:10
  438.2 134.9 %all-gather.29.cloned.1.call-start = ((), (), s32[]{:S(2)}) async-start(), calls=%async_computation.8 | async-start | bytes 2359296 | tf_op jit(solution)/shard_map/all_gather | solution.py:47
  477.5 50.7 %collective-permute-start.6 = (bf16[4,2,128,1024]{3,2,0,1:T(8,128)(2,1)}, bf16[4,2,128,1024]{3,2,0,1:T(8,128)(2,1)}, u32[]{:S(2)}, u32[]{:S(2)}) collective-permute-start(bf16[4,2,128,1024]{3,2,0,1:T(8,128)(2,1)} %all-gather.27.cloned.1.call-done), channel_id=1, source_target_pairs={{0,16},{8,24},{16,32},{24,40},{32,48},{40,56},{48,64},{56,72},{64,... | collective-permute-start | bytes 6291464 | tf_op jit(solution)/shard_map/ppermute | solution.py:10
  528.4 0.8 copy-start.18
  531.1 133.8 %all-gather.31.cloned.1.call-start = ((), (), s32[]{:S(2)}) async-start(), calls=%async_computation.9 | async-start | bytes 2359296 | tf_op jit(solution)/shard_map/all_gather | solution.py:95
  573.1 49.2 %collective-permute-start.7 = (bf16[4,2,128,1024]{3,2,0,1:T(8,128)(2,1)}, bf16[4,2,128,1024]{3,2,0,1:T(8,128)(2,1)}, u32[]{:S(2)}, u32[]{:S(2)}) collective-permute-start(bf16[4,2,128,1024]{3,2,0,1:T(8,128)(2,1)} %all-gather.29.cloned.1.call-done), channel_id=1, source_target_pairs={{0,8},{8,16},{16,24},{24,32},{32,40},{40,48},{48,56},{56,64},{64,7... | collective-permute-start | bytes 6291464 | tf_op jit(solution)/shard_map/ppermute | solution.py:10
  622.2 2.2 copy-start.6
  624.4 1.9 copy-start.26
  626.8 1.6 copy-start.14
  635.8 1.6 copy-start
  637.4 1.6 copy-start.31
  664.8 1.9 copy-start.33
  667.6 1.0 copy-start.29
  667.6 1.1 copy-start.16
Sparse Core Ops, SparseCore 0:
  9.0 29.9 all-gather.32
  44.9 28.2 all-gather.12
  96.5 28.8 all-gather.14
  143.9 34.0 all-gather.16
  194.3 30.4 all-gather.18
  242.5 27.5 all-gather.20
  271.8 28.2 all-gather.22
  350.6 37.4 all-gather.24
  438.3 39.1 all-gather.26
  531.2 41.8 all-gather.28
  636.0 28.8 all-gather.30
where the time goes:
time: 678 us; the launch traced here: 676 us
  waiting for transfers between devices  575 us (85%)
  matrix products  26.3 us (4%)
  local copies, waits for them, and re-layouts  25.8 us (4%)
  starting transfers between devices  22.9 us (3%)
  between operations  13.6 us (2%)
  other arithmetic  11.9 us (2%)
    ppermute x8, waiting for transfers between devices, from_behind(): lax.ppermute(value, axis, [(source, source + steps) for source in range(l...  237 us
    all_gather x6, waiting for transfers between devices, gather_rhs(): lax.all_gather(panel_shard.astype(jnp.bfloat16), 'col', axis=3, tiled=True)  168 us
    all_gather x4, waiting for transfers between devices, bring_lower(): gathered = lax.all_gather(pieces, 'col', axis=3, tiled=True)  148 us
    all_gather x1, waiting for transfers between devices, local(): lax.all_gather(solved[member - stride].astype(jnp.bfloat16), 'col', axis=...  22.5 us
    ppermute x8, starting transfers between devices, from_behind(): lax.ppermute(value, axis, [(source, source + steps) for source in range(l...  22.4 us
    unnamed x33, local copies, waits for them, and re-layouts  14.1 us
  transfers between devices with their start and end apart: 19, of which 19 were waited for; matrix products, arithmetic and copies ran while one was open for 3% of the time, Pallas kernels for 0%

commit v1 on v0

v1 whole, which is shorter than its diff:
```python
import functools

import jax
import jax.numpy as jnp
from jax import lax
from jax.experimental import pallas as pl
from jax.experimental.pallas import tpu as pltpu
from jax.sharding import PartitionSpec as P

MESH = pl.DeviceIdType.MESH
BF16 = jnp.bfloat16
F32 = jnp.float32
CHIPS = 4
CUTS = 4
LAG = 3
C0_ODD, C0_EVEN, I_EVEN, I_ODD, C1_EVEN, C1_ODD = range(6)


def kernel(
    force, inverse, coupling, out,
    fac, odd_v, even_f, base, red, upd, upd_out, inv_even, inv_odd, low, own, stage, acc,
    fac_sem, odd_sem, even_sem, base_sem, upd_sem, low_sem, own_sem, out_sem,
    fac_sent, odd_sent, even_sent, base_sent, upd_sent, low_sent, own_sent, out_sent, out_kept,
):
    chunks = base.shape[0]
    rhs = force.shape[3]
    cut = rhs // CUTS
    half = rhs // 2
    p = lax.axis_index("radial")
    c = lax.axis_index("col")
    z = lax.div(c, 2)
    k = lax.rem(c, 2)
    other = 1 - k
    levels = 4
    height = jnp.where(
        lax.rem(p, 2) == 1, 0,
        jnp.where(lax.rem(p, 4) == 2, 1, jnp.where(lax.rem(p, 8) == 4, 2, jnp.where(p == 8, 3, 4))),
    )
    reach = jnp.where(height == 0, 1, jnp.where(height == 1, 2, jnp.where(height == 2, 4, 8)))
    top = p == 0
    below = jnp.where(top, 0, p - reach)

    def ring(step):
        return lax.rem(z + step, CHIPS)

    def remote(src, dst, sent, got, column, target):
        copy = pltpu.make_async_remote_copy(
            src_ref=src, dst_ref=dst, send_sem=sent, recv_sem=got,
            device_id=(column, target), device_id_type=MESH,
        )
        copy.start()

    def local(src, dst, sem):
        pltpu.make_async_copy(src, dst, sem).start()

    def await_bytes(ref, sem):
        pltpu.make_async_copy(ref, ref, sem).wait()

    def factor(which, freq):
        if which == I_EVEN or which == I_ODD:
            return inverse.at[freq, which - I_EVEN]
        row = {C0_ODD: 1, C0_EVEN: 0, C1_EVEN: 0, C1_ODD: 1}[which]
        return coupling.at[freq, row, 0 if which < I_EVEN else 1]

    for which in (C0_ODD, C0_EVEN, I_EVEN, I_ODD, C1_EVEN, C1_ODD):
        for g in range(2):
            local(factor(which, 2 * k + g), fac.at[which, g, k], fac_sem.at[which, g])
        if which == C0_ODD:
            local(force.at[pl.ds(2 * k, 2), 0], even_f.at[k], even_sem)
            for g in range(2):
                for h in range(2):
                    local(
                        force.at[2 * k + g, 1, :, pl.ds(h * half, half)],
                        odd_v.at[g, h, c], odd_sem.at[g, h],
                    )

    barrier = pltpu.get_barrier_semaphore()

    def greet(column, target):
        pl.semaphore_signal(barrier, inc=1, device_id=(column, target), device_id_type=MESH)

    for step in range(1, CHIPS):
        for core in range(2):
            greet(p, 2 * ring(step) + core)
    greet(p, 2 * z + other)

    @pl.when(p > 0)
    def _():
        for chip in range(CHIPS):
            greet(below, 2 * chip + k)

    for level in range(levels):
        @pl.when(level < height)
        def _():
            for chip in range(CHIPS):
                greet(p + 2**level, 2 * chip + k)

    pl.semaphore_wait(barrier, 7 + CHIPS * (height + jnp.where(top, 0, 1)))

    def lend(which):
        for g in range(2):
            remote(
                factor(which, 2 * other + g), fac.at[which, g, k], fac_sent, fac_sem.at[which, g],
                p, 2 * z + other,
            )

    lend(C0_ODD)
    remote(force.at[pl.ds(2 * other, 2), 0], even_f.at[k], even_sent, even_sem, p, 2 * z + other)
    for g in range(2):
        for h in range(2):
            for step in (1, 3, 2, 0):
                for core in range(2):
                    def send():
                        remote(
                            force.at[2 * core + g, 1, :, pl.ds(h * half, half)],
                            odd_v.at[g, h, c], odd_sent, odd_sem.at[g, h], p, 2 * ring(step) + core,
                        )
                    if step:
                        send()
                    else:
                        pl.when(core != k)(send)
    for which in (C0_EVEN, I_EVEN, I_ODD, C1_EVEN, C1_ODD):
        lend(which)

    def times(panel, which, g):
        wide = jnp.concatenate(
            [fac[which, g, 0, 0], fac[which, g, 1, 0], fac[which, g, 0, 1], fac[which, g, 1, 1]], axis=1
        )
        both = jnp.dot(panel, wide, preferred_element_type=F32)
        n = wide.shape[1] // 2
        real = both[:cut, :n] + both[cut:, n:]
        imag = both[cut:, :n] - both[:cut, n:]
        return jnp.concatenate([real, imag], axis=0)

    def across(ref, i):
        return jnp.concatenate([ref[i, chip] for chip in range(CHIPS)], axis=1)

    def place(i):
        g = lax.div(i, CUTS)
        q = lax.rem(i, CUTS)
        h = lax.div(q, CUTS // 2)
        r = lax.rem(q, CUTS // 2)
        return g, q, h, pl.multiple_of(r * cut, cut)

    def odd_panel(i):
        g, _, h, r = place(i)
        parts = [
            jnp.concatenate([odd_v[g, h, col, part, pl.ds(r, cut)] for col in range(2 * CHIPS)], axis=1)
            for part in range(2)
        ]
        return jnp.concatenate(parts, axis=0)

    def write_out(i, row, value):
        g, q, _, _ = place(i)
        at = pl.ds(pl.multiple_of(q * cut, cut), cut)
        for side in range(2):
            for part in range(2):
                stage[side, g, row, part, at] = value[part * cut:(part + 1) * cut, side * 128:(side + 1) * 128]
        local(stage.at[k, g, row, :, at], out.at[2 * k + g, row, :, at], out_kept)
        remote(
            stage.at[other, g, row, :, at], out.at[2 * k + g, row, :, at], out_sent, out_sem,
            p, 2 * z + other,
        )

    def reduce_odd(i):
        g, q, h, r = place(i)

        @pl.when(lax.rem(q, CUTS // 2) == 0)
        def _():
            await_bytes(odd_v.at[g, h], odd_sem.at[g, h])

        at = pl.ds(pl.multiple_of(q * cut, cut), cut)
        mine = jnp.concatenate(
            [
                jnp.concatenate([even_f[side, g, part, at] for side in range(2)], axis=1)
                for part in range(2)
            ],
            axis=0,
        )
        left = mine.astype(F32) - times(odd_panel(i), C0_ODD, g)
        base[i, z] = left.astype(BF16)
        for step in (1, 3, 2):
            remote(base.at[i, z], base.at[i, z], base_sent, base_sem.at[i], p, 2 * ring(step) + k)

    def solved(i, value):
        own[i, z] = value.astype(BF16)
        for level in range(levels):
            @pl.when(height == level + 1)
            def _():
                for chip in range(CHIPS):
                    remote(
                        own.at[i, z], low.at[i, z], low_sent.at[level], low_sem.at[i],
                        p + 2**level, 2 * chip + k,
                    )
        for step in (1, 3, 2):
            remote(own.at[i, z], own.at[i, z], own_sent, own_sem.at[i], p, 2 * ring(step) + k)
        write_out(i, 0, value)

    def reduce_even(i):
        g, _, _, _ = place(i)
        await_bytes(base.at[i, pl.ds(0, 3)], base_sem.at[i])

        @pl.when(height == 0)
        def _():
            red[i] = base[i]

        for level in range(levels):
            @pl.when(level < height)
            def _():
                await_bytes(upd.at[level, i], upd_sem.at[level, i])
                before = base[i].astype(F32) if level == 0 else acc[...]
                acc[...] = before - upd[level, i].astype(F32)

        @pl.when(height > 0)
        def _():
            red[i] = acc[...].astype(BF16)

        product = times(across(red, i), jnp.where(top, I_EVEN, C0_EVEN), g)

        @pl.when(p > 0)
        def _():
            upd_out[i] = product.astype(BF16)
            for chip in range(CHIPS):
                remote(
                    upd_out.at[i], upd.at[height, i, z], upd_sent, upd_sem.at[height, i],
                    below, 2 * chip + k,
                )

        @pl.when(top)
        def _():
            solved(i, product)

    def apply_inverses(i):
        g, _, _, _ = place(i)
        inv_odd[i] = times(odd_panel(i), I_ODD, g)

        @pl.when(p > 0)
        def _():
            inv_even[i] = times(across(red, i), I_EVEN, g)

    def back_even(i):
        g, _, _, _ = place(i)
        await_bytes(low.at[i], low_sem.at[i])
        solved(i, inv_even[i] - times(across(low, i), C1_EVEN, g))

    def back_odd(i):
        g, _, _, _ = place(i)
        await_bytes(own.at[i, pl.ds(0, 3)], own_sem.at[i])
        for level in reversed(range(levels - 1)):
            @pl.when(level + 1 < height)
            def _():
                remote(
                    own.at[i], low.at[i], low_sent.at[level], low_sem.at[i], p + 2**level, c
                )
        write_out(i, 1, inv_odd[i] - times(across(own, i), C1_ODD, g))

    leaf = height == 0
    at_even = jnp.where(leaf, LAG, chunks)
    at_inverse = jnp.where(leaf, LAG + chunks, chunks)
    at_back = jnp.where(leaf, LAG + chunks, chunks) + chunks
    at_odd = jnp.where(top, at_even, at_back) + LAG

    for g in range(2):
        await_bytes(fac.at[C0_ODD, g], fac_sem.at[C0_ODD, g])
    await_bytes(even_f, even_sem)

    def step(s, _):
        @pl.when(s < chunks)
        def _():
            reduce_odd(s)

        def during(start, work, needs=()):
            i = s - start

            @pl.when(jnp.logical_and(i >= 0, i < chunks))
            def _():
                for which, here in needs:
                    @pl.when(jnp.logical_and(i == 0, here))
                    def _():
                        for g in range(2):
                            await_bytes(fac.at[which, g], fac_sem.at[which, g])
                work(i)

        during(at_even, reduce_even, ((C0_EVEN, True), (I_EVEN, top)))
        during(
            at_inverse, apply_inverses,
            ((I_EVEN, p > 0), (I_ODD, True), (C1_EVEN, True), (C1_ODD, True)),
        )

        @pl.when(p > 0)
        def _():
            during(at_back, back_even)

        during(at_odd, back_odd)
        return 0

    lax.fori_loop(0, 3 * chunks + 2 * LAG, step, 0)

    await_bytes(fac.at[pl.ds(0, 3)], fac_sent)
    await_bytes(odd_v.at[:, :, pl.ds(0, 7)], odd_sent)
    await_bytes(even_f.at[0], even_sent)
    await_bytes(base.at[:, pl.ds(0, 3)], base_sent)
    await_bytes(own.at[:, pl.ds(0, 3)], own_sent)

    @pl.when(p > 0)
    def _():
        await_bytes(base, upd_sent)

    for level in range(levels):
        @pl.when(level < height)
        def _():
            await_bytes(low, low_sent.at[level])
    await_bytes(stage.at[0], out_kept)
    await_bytes(stage.at[0], out_sent)
    await_bytes(stage.at[0], out_sem)


def local_solve(force, inverse, coupling):
    freqs, _, _, rhs, cols = force.shape
    block = inverse.shape[3]
    chunks = 2 * CUTS
    rows = 2 * rhs // CUTS
    wide = 2 * cols
    dma = pltpu.SemaphoreType.DMA
    panel = (chunks, CHIPS, rows, wide)
    hbm = pl.BlockSpec(memory_space=pl.ANY)
    return pl.pallas_call(
        kernel,
        out_shape=jax.ShapeDtypeStruct(force.shape, F32),
        in_specs=[hbm] * 3,
        out_specs=hbm,
        scratch_shapes=[
            pltpu.VMEM((6, 2, 2, 2, block, cols), BF16),
            pltpu.VMEM((2, 2, 2 * CHIPS, 2, rhs // 2, cols), BF16),
            pltpu.VMEM((2, 2, 2, rhs, cols), BF16),
            pltpu.VMEM(panel, BF16),
            pltpu.VMEM(panel, BF16),
            pltpu.VMEM((4,) + panel, BF16),
            pltpu.VMEM((chunks, rows, wide), BF16),
            pltpu.VMEM((chunks, rows, wide), F32),
            pltpu.VMEM((chunks, rows, wide), F32),
            pltpu.VMEM(panel, BF16),
            pltpu.VMEM(panel, BF16),
            pltpu.VMEM((2, 2, 2, 2, rhs, cols), F32),
            pltpu.VMEM(panel[1:], F32),
            dma((6, 2)), dma((2, 2)), dma, dma((chunks,)), dma((4, chunks)), dma((chunks,)), dma((chunks,)), dma,
            dma, dma, dma, dma, dma, dma((4,)), dma, dma, dma,
        ],
        compiler_params=pltpu.CompilerParams(
            collective_id=0, has_side_effects=True, vmem_limit_bytes=48 * 2**20
        ),
        name="resolvent",
    )(force, inverse, coupling)


def solution(mesh):
    return jax.shard_map(
        local_solve,
        mesh=mesh,
        in_specs=(
            P(None, "radial", None, None, "col"),
            P(None, "radial", None, None, "col"),
            P(None, "radial", None, None, None, "col"),
        ),
        out_specs=P(None, "radial", None, None, "col"),
        check_vma=False,
    )
```

time: 678 us -> 146 us (0.22)
  waiting for transfers between devices: 575 us -> 0 us
  Pallas kernels: 0 us -> 141 us
  matrix products: 26.3 us -> 0 us
  starting transfers between devices: 22.9 us -> 0 us
  local copies, waits for them, and re-layouts: 25.8 us -> 4.2 us
  between operations: 13.6 us -> 0.01 us
  other arithmetic: 11.9 us -> 0 us
    all_gather x11 -> x0, waiting for transfers between devices: 339 us -> none  [the longest x6 168 us: gather_rhs(): lax.all_gather(panel_shard.astype(jnp.bfloat16), 'col', axis=3, tiled=True)]
    ppermute x8 -> x0, waiting for transfers between devices: 237 us -> none  [from_behind(): lax.ppermute(value, axis, [(source, source + steps) for source in range(l...]
    pallas_call x0 -> x1, Pallas kernels: none -> 141 us  [local_solve(): pl.pallas_call(kernel, out_shape=jax.ShapeDtypeStruct(force.shape, F32),...]
    dot_general x24 -> x0, matrix products: 26.3 us -> none  [the longest x6 10.2 us: conj_product(): jnp.einsum('frk,fkn->frn', gathered[:, 1], factor[:, 0], preferred_elemen...]
    ppermute x8 -> x0, starting transfers between devices: 22.4 us -> none  [from_behind(): lax.ppermute(value, axis, [(source, source + steps) for source in range(l...]
    unnamed x33 -> x5, local copies, waits for them, and re-layouts: 14.1 us -> 4.2 us
    slice x3 -> x0, local copies, waits for them, and re-layouts: 8.8 us -> none  [the longest x1 5.23 us: local(): couplings[:, member, 1]]
    convert_element_type x10 -> x0, other arithmetic: 8.8 us -> none  [the longest x4 4.12 us: bring_lower(): pieces = panel_shard.astype(jnp.bfloat16)]
  transfers between devices with their start and end apart: 19 -> 0, of which waited for: 19 -> 0; matrix products, arithmetic and copies ran while one was open for 3% -> 0% of each run, Pallas kernels for 0% -> 0%
where the time goes in v1:
time: 146 us; the launch traced here: 145 us
  Pallas kernels  141 us (97%)
  local copies, waits for them, and re-layouts  4.2 us (3%)
    pallas_call x1, Pallas kernels, local_solve(): pl.pallas_call(kernel, out_shape=jax.ShapeDtypeStruct(force.shape, F32),...  141 us
    unnamed x5, local copies, waits for them, and re-layouts  4.2 us

profile of v1, /device:TPU:27, one launch (start us, length us, event | category | flops | bytes accessed | tf_op | source)
XLA Modules:
  0.0 145.2 jit_solution(2427293812058373798)
XLA Ops:
  0.0 0.0 copy-start
  0.0 2.2 %copy-done = bf16[4,2,2,1024,128]{4,3,2,1,0:T(8,128)(2,1)S(1)} copy-done((bf16[4,2,2,1024,128]{4,3,2,1,0:T(8,128)(2,1)S(1)}, bf16[4,2,2,1024,128]{4,3,2,1,0:T(8,128)(2,1)}, u32[]{:S(2)}) %copy-start) | copy-done | bytes 4194328
  2.2 0.0 copy-start.1
  2.2 1.0 copy-done.1
  3.2 141.0 %resolvent.1 = f32[4,2,2,128,128]{4,3,2,1,0:T(8,128)S(1)} custom-call(bf16[4,2,2,128,128]{4,3,2,1,0:T(8,128)(2,1)S(1)} %copy-done.1, bf16[4,2,2,1024,128]{4,3,2,1,0:T(8,128)(2,1)S(1)} %copy-done, bf16[4,2,2,2,1024,128]{5,4,3,2,1,0:T(8,128)(2,1)} %coupling.1), custom_call_target="tpu_custom_call" | custom-call | tf_op jit(solution)/shard_map/resolvent/pallas_call | solution.py:327
  144.2 1.0 copy.5
Async XLA Ops:
  0.0 2.2 %copy-start = (bf16[4,2,2,1024,128]{4,3,2,1,0:T(8,128)(2,1)S(1)}, bf16[4,2,2,1024,128]{4,3,2,1,0:T(8,128)(2,1)}, u32[]{:S(2)}) copy-start(bf16[4,2,2,1024,128]{4,3,2,1,0:T(8,128)(2,1)} %inverse.1) | copy-start | bytes 12582916
  2.2 1.0 copy-start.1

commit v2 on v1

v2 whole, which is shorter than its diff:
```python
import jax
import jax.numpy as jnp
from jax import lax
from jax.experimental import pallas as pl
from jax.experimental.pallas import tpu as pltpu
from jax.sharding import PartitionSpec as P

MESH = pl.DeviceIdType.MESH
BF16 = jnp.bfloat16
F32 = jnp.float32
CHIPS = 4
CUTS = 4
C0, INV, C1 = range(3)
MIDDLE = 3
SETTLE = 2


def kernel(
    force, inverse, coupling, out,
    fac, mid, upp, odd_v, even_f, base, shard, mid_out, up_base, up_mid, up_all, up_upd, up_out, up_red,
    up_inv, up_low, up_own, inv_even, inv_odd, low, own, stage, up_stage, acc,
    fac_sem, mid_sem, upp_sem, odd_sem, even_sem, base_sem, up_base_sem, up_mid_sem, up_all_sem, up_upd_sem,
    up_low_sem, up_own_sem, low_sem, own_sem, out_sem, out_core_sem, out_far_sem,
    fac_sent, mid_sent, upp_lent, upp_sent, odd_sent, even_sent, base_sent, shard_sent, mid_out_sent,
    up_all_sent, up_out_sent, up_first_sent, up_own_sent, full_sent, own_sent, out_sent, out_kept,
    up_stage_sent, up_stage_kept,
):
    chunks = base.shape[0]
    rhs = force.shape[3]
    cut = rhs // CUTS
    half = rhs // 2
    p = lax.axis_index("radial")
    c = lax.axis_index("col")
    x, y = lax.div(p, 4), lax.rem(p, 4)
    z, k = lax.div(c, 2), lax.rem(c, 2)
    other = 1 - k
    odd = lax.rem(y, 2) == 1
    even = lax.rem(y, 2) == 0
    kind_a = jnp.logical_or(y == 0, jnp.logical_and(odd, y == 1 + 2 * k))
    kind_b = jnp.logical_not(kind_a)
    up_g = lax.rem(y, 2)
    home = 4 * x + jnp.where(kind_a, 0, 2)
    height = jnp.where(kind_b, 0, jnp.where(lax.rem(x, 2) == 1, 1, jnp.where(x == 2, 2, 3)))
    top = height == 3
    inner = height < 3
    twin = 4 * x + lax.rem(y + 2, 4)
    parent = jnp.where(kind_b, twin, jnp.where(height == 1, p - 4, jnp.where(height == 2, p - 8, p)))
    first = jnp.where(height == 3, p + 8, jnp.where(height == 2, p + 4, twin))
    beside = 4 * x + lax.rem(y + 1 + 2 * k, 4)
    child = 4 * x + jnp.where(kind_a, 1, 3)
    child_here = child == p

    def both(one, two):
        return jnp.logical_and(one, two)

    def ring(step):
        return lax.rem(z + step, CHIPS)

    def remote(src, dst, sent, got, column, target):
        pltpu.make_async_remote_copy(
            src_ref=src, dst_ref=dst, send_sem=sent, recv_sem=got,
            device_id=(column, target), device_id_type=MESH,
        ).start()

    def local(src, dst, sem):
        pltpu.make_async_copy(src, dst, sem).start()

    def await_bytes(ref, sem):
        pltpu.make_async_copy(ref, ref, sem).wait()

    def factor(which, row, freq):
        if which == INV:
            return inverse.at[freq, row]
        return coupling.at[freq, row, 0 if which == C0 else 1]

    def keep(which, row, ref, sem):
        for g in range(2):
            local(factor(which, row, 2 * k + g), ref.at[which, g, k], sem.at[which, g])

    def lend(which, row, ref, sem, sent):
        for g in range(2):
            remote(
                factor(which, row, 2 * other + g), ref.at[which, g, k], sent, sem.at[which, g],
                p, 2 * z + other,
            )

    keep(C0, 1, fac, fac_sem)
    local(force.at[pl.ds(2 * k, 2), 0], even_f.at[k], even_sem)
    for g in range(2):
        for h in range(2):
            local(
                force.at[2 * k + g, 1, :, pl.ds(h * half, half)], odd_v.at[g, h, c], odd_sem.at[g, h]
            )
    for which in (C0, INV, C1):
        @pl.when(odd)
        def _():
            keep(which, 0, mid, mid_sem)

        @pl.when(even)
        def _():
            local(factor(which, 0, 2 * k), upp.at[which, k], upp_sem.at[which])

        if which != C0:
            keep(which, 1, fac, fac_sem)

    barrier = pltpu.get_barrier_semaphore()

    def greet(column, target):
        pl.semaphore_signal(barrier, inc=1, device_id=(column, target), device_id_type=MESH)

    for step in range(1, CHIPS):
        for core in range(2):
            greet(p, 2 * ring(step) + core)
    greet(p, 2 * z + other)
    for core in range(2):
        greet(4 * x + lax.rem(y + 1, 4), 2 * z + core)
        greet(4 * x + lax.rem(y + 3, 4), 2 * z + core)
    for chip in range(CHIPS):
        greet(twin, 2 * chip + k)

    @pl.when(y >= 2)
    def _():
        for step in range(1, CHIPS):
            greet(4 * x + 5 - y, 2 * ring(step) + k)

    def greet_chips(column):
        for chip in range(CHIPS):
            greet(column, 2 * chip + k)

    a_even = both(kind_a, lax.rem(x, 2) == 0)

    @pl.when(both(kind_a, height < 3))
    def _():
        greet_chips(parent)

    @pl.when(a_even)
    def _():
        greet_chips(p + 4)

    @pl.when(top)
    def _():
        greet_chips(p + 8)

    pl.semaphore_wait(
        barrier,
        15 + jnp.where(y >= 2, 3, 0) + jnp.where(kind_a, jnp.where(lax.rem(x, 2) == 0, 8, 4), 0),
    )

    lend(C0, 1, fac, fac_sem, fac_sent)
    remote(force.at[pl.ds(2 * other, 2), 0], even_f.at[k], even_sent, even_sem, p, 2 * z + other)
    for g in range(2):
        for h in range(2):
            for step in (1, 3, 2, 0):
                for core in range(2):
                    def send():
                        remote(
                            force.at[2 * core + g, 1, :, pl.ds(h * half, half)],
                            odd_v.at[g, h, c], odd_sent, odd_sem.at[g, h], p, 2 * ring(step) + core,
                        )
                    if step:
                        send()
                    else:
                        pl.when(core != k)(send)
    for which in (C0, INV, C1):
        @pl.when(odd)
        def _():
            lend(which, 0, mid, mid_sem, mid_sent)

        @pl.when(even)
        def _():
            for core in range(2):
                remote(
                    factor(which, 0, 2 * core + 1), upp.at[which, k], upp_sent, upp_sem.at[which],
                    4 * x + lax.rem(y + 1 + 2 * core, 4), 2 * z + core,
                )
            remote(
                factor(which, 0, 2 * other), upp.at[which, k], upp_lent, upp_sem.at[which],
                p, 2 * z + other,
            )

        if which != C0:
            lend(which, 1, fac, fac_sem, fac_sent)

    def times(panel, ref):
        wide = jnp.concatenate([ref[0, 0], ref[1, 0], ref[0, 1], ref[1, 1]], axis=1)
        product = jnp.dot(panel, wide, preferred_element_type=F32)
        n = wide.shape[1] // 2
        real = product[:cut, :n] + product[cut:, n:]
        imag = product[cut:, :n] - product[:cut, n:]
        return jnp.concatenate([real, imag], axis=0)

    def across(ref, i):
        return jnp.concatenate([ref[i, chip] for chip in range(CHIPS)], axis=1)

    def place(i):
        g = lax.div(i, CUTS)
        q = lax.rem(i, CUTS)
        h = lax.div(q, CUTS // 2)
        r = lax.rem(q, CUTS // 2)
        return g, q, h, pl.multiple_of(r * cut, cut)

    def rows_of(q):
        return pl.ds(pl.multiple_of(q * cut, cut), cut)

    def odd_panel(i):
        g, _, h, r = place(i)
        parts = [
            jnp.concatenate([odd_v[g, h, col, part, pl.ds(r, cut)] for col in range(2 * CHIPS)], axis=1)
            for part in range(2)
        ]
        return jnp.concatenate(parts, axis=0)

    def along(ref, i, sent, sem):
        for step in (1, 3, 2):
            remote(ref.at[i, z], ref.at[i, z], sent, sem.at[i], p, 2 * ring(step) + k)

    def straight(src, dst, sent, got, column):
        for chip in range(CHIPS):
            remote(src, dst, sent, got, column, 2 * chip + k)

    def write_out(i, row, value):
        g, q, _, _ = place(i)
        at = rows_of(q)
        for side in range(2):
            for part in range(2):
                stage[side, g, row, part, at] = value[part * cut:(part + 1) * cut, side * 128:(side + 1) * 128]
        local(stage.at[k, g, row, :, at], out.at[2 * k + g, row, :, at], out_kept)
        remote(
            stage.at[other, g, row, :, at], out.at[2 * k + g, row, :, at], out_sent, out_sem,
            p, 2 * z + other,
        )

    def write_upper(j, value):
        at = rows_of(j)
        freq = 2 * k + up_g
        for side in range(2):
            for part in range(2):
                up_stage[side, part, at] = value[part * cut:(part + 1) * cut, side * 128:(side + 1) * 128]

        @pl.when(even)
        def _():
            local(up_stage.at[k, :, at], out.at[freq, 0, :, at], up_stage_kept)
            remote(
                up_stage.at[other, :, at], out.at[freq, 0, :, at], up_stage_sent, out_core_sem,
                p, 2 * z + other,
            )

        @pl.when(odd)
        def _():
            for side in range(2):
                remote(
                    up_stage.at[side, :, at], out.at[freq, 0, :, at], up_stage_sent, out_far_sem,
                    home, 2 * z + side,
                )

    def await_factor(ref, which, sem):
        for g in range(2):
            await_bytes(ref.at[which, g], sem.at[which, g])

    def await_upper(which):
        await_bytes(upp.at[which], upp_sem.at[which])

    def once(i, work):
        pl.when(i == 0)(work)

    def reduce_odd(i):
        g, q, h, _ = place(i)

        @pl.when(lax.rem(q, CUTS // 2) == 0)
        def _():
            await_bytes(odd_v.at[g, h], odd_sem.at[g, h])

        at = rows_of(q)
        mine = jnp.concatenate(
            [
                jnp.concatenate([even_f[side, g, part, at] for side in range(2)], axis=1)
                for part in range(2)
            ],
            axis=0,
        )
        left = (mine.astype(F32) - times(odd_panel(i), fac.at[C0, g])).astype(BF16)

        @pl.when(odd)
        def _():
            base[i, z] = left
            along(base, i, base_sent, base_sem)

        @pl.when(both(even, g == 0))
        def _():
            up_base[q] = left

        @pl.when(both(even, g == 1))
        def _():
            shard[q] = left
            remote(shard.at[q], up_base.at[q], shard_sent, up_base_sem.at[q], beside, c)

    def reduce_middle(i):
        g, q, _, _ = place(i)
        once(i, lambda: await_factor(mid, C0, mid_sem))
        await_bytes(base.at[i, pl.ds(0, 3)], base_sem.at[i])
        mid_out[i] = times(across(base, i), mid.at[C0, g]).astype(BF16)

        @pl.when(g == 0)
        def _():
            remote(mid_out.at[i], up_mid.at[q], mid_out_sent, up_mid_sem.at[q], p - 1, c)

        @pl.when(both(g == 1, k == 0))
        def _():
            local(mid_out.at[i], up_mid.at[q], up_mid_sem.at[q])

        @pl.when(both(g == 1, k == 1))
        def _():
            remote(mid_out.at[i], up_mid.at[q], mid_out_sent, up_mid_sem.at[q], twin, c)

    def inverse_odd(i):
        g, _, _, _ = place(i)
        once(i, lambda: await_factor(fac, INV, fac_sem))
        inv_odd[i] = times(odd_panel(i), fac.at[INV, g])

    def inverse_middle(i):
        g, _, _, _ = place(i)
        once(i, lambda: await_factor(mid, INV, mid_sem))
        inv_even[i] = times(across(base, i), mid.at[INV, g])

    def settle_upper(j):
        @pl.when(odd)
        def _():
            await_bytes(up_base.at[j], up_base_sem.at[j])

        await_bytes(up_mid.at[j], up_mid_sem.at[j])
        up_all[j, z] = (up_base[j].astype(F32) - up_mid[j].astype(F32)).astype(BF16)
        along(up_all, j, up_all_sent, up_all_sem)

    def reduce_upper(j):
        @pl.when(j == 0)
        def _():
            await_upper(C0)

            @pl.when(top)
            def _():
                await_upper(INV)
                await_upper(C1)

        await_bytes(up_all.at[j, pl.ds(0, 3)], up_all_sem.at[j])

        @pl.when(height == 0)
        def _():
            up_red[j] = up_all[j]

        for level in range(3):
            @pl.when(level < height)
            def _():
                await_bytes(up_upd.at[level, j], up_upd_sem.at[level, j])
                before = up_all[j].astype(F32) if level == 0 else acc[...]
                acc[...] = before - up_upd[level, j].astype(F32)

        @pl.when(height > 0)
        def _():
            up_red[j] = acc[...].astype(BF16)

        product = times(across(up_red, j), upp.at[jnp.where(top, INV, C0)])

        @pl.when(inner)
        def _():
            up_out[j] = product.astype(BF16)
            straight(up_out.at[j], up_upd.at[height, j, z], up_out_sent, up_upd_sem.at[height, j], parent)

        @pl.when(top)
        def _():
            solved_upper(j, product)

    def inverse_upper(j):
        once(j, lambda: await_upper(INV))
        up_inv[j] = times(across(up_red, j), upp.at[INV])

    def solved_upper(j, value):
        up_own[j, z] = value.astype(BF16)

        @pl.when(height > 0)
        def _():
            straight(up_own.at[j, z], up_low.at[j, z], up_first_sent, up_low_sem.at[j], first)

        @pl.when(both(kind_b, jnp.logical_not(child_here)))
        def _():
            i = up_g * CUTS + j
            straight(up_own.at[j, z], low.at[i, z], up_first_sent, low_sem.at[i], child)

        along(up_own, j, up_own_sent, up_own_sem)
        write_upper(j, value)

    def pass_upper(j):
        i = up_g * CUTS + j
        await_bytes(up_own.at[j, pl.ds(0, 3)], up_own_sem.at[j])

        @pl.when(child_here)
        def _():
            local(up_own.at[j], low.at[i], low_sem.at[i])

        @pl.when(top)
        def _():
            remote(up_own.at[j], up_low.at[j], full_sent.at[0], up_low_sem.at[j], p + 4, c)

        @pl.when(a_even)
        def _():
            remote(up_own.at[j], up_low.at[j], full_sent.at[1], up_low_sem.at[j], twin, c)

        @pl.when(both(kind_a, jnp.logical_not(child_here)))
        def _():
            remote(up_own.at[j], low.at[i], full_sent.at[2], low_sem.at[i], child, c)

        @pl.when(odd)
        def _():
            remote(up_own.at[j], own.at[i], full_sent.at[3], own_sem.at[i], home, c)

    def back_upper(j):
        once(j, lambda: await_upper(C1))
        await_bytes(up_low.at[j], up_low_sem.at[j])
        solved_upper(j, up_inv[j] - times(across(up_low, j), upp.at[C1]))

    def back_middle(i):
        g, _, _, _ = place(i)
        once(i, lambda: await_factor(mid, C1, mid_sem))
        await_bytes(low.at[i], low_sem.at[i])
        value = inv_even[i] - times(across(low, i), mid.at[C1, g])
        own[i, z] = value.astype(BF16)
        along(own, i, own_sent, own_sem)
        write_out(i, 0, value)

    def back_odd(i):
        g, q, _, _ = place(i)
        once(i, lambda: await_factor(fac, C1, fac_sem))

        @pl.when(odd)
        def _():
            await_bytes(own.at[i, pl.ds(0, 3)], own_sem.at[i])

        @pl.when(both(even, g == 0))
        def _():
            own[i] = up_own[q]

        @pl.when(both(even, g == 1))
        def _():
            await_bytes(own.at[i], own_sem.at[i])

        write_out(i, 1, inv_odd[i] - times(across(own, i), fac.at[C1, g]))

    at_settle = jnp.where(even, MIDDLE + 3, MIDDLE + 7)
    at_upper = at_settle + jnp.where(kind_b, SETTLE, CUTS)
    at_middle_inverse = MIDDLE + 7 + 2 * CUTS
    at_back = at_middle_inverse + chunks
    at_pass = jnp.where(top, at_upper, at_back) + SETTLE
    at_end = at_back + 3

    for g in range(2):
        await_bytes(fac.at[C0, g], fac_sem.at[C0, g])
    await_bytes(even_f, even_sem)

    def step(s, _):
        def during(start, count, work, who=None):
            i = s - start
            now = both(i >= 0, i < count)

            @pl.when(now if who is None else both(now, who))
            def _():
                work(i)

        during(0, chunks, reduce_odd)
        during(MIDDLE, chunks, reduce_middle, odd)
        during(MIDDLE + 1, chunks, inverse_odd)
        during(at_settle, CUTS, settle_upper)
        during(at_upper, CUTS, reduce_upper)
        during(at_upper, CUTS, inverse_upper, inner)
        during(at_middle_inverse, chunks, inverse_middle, odd)
        during(at_back, CUTS, back_upper, inner)
        during(at_pass, CUTS, pass_upper)
        during(at_back, chunks, back_middle, odd)
        during(at_end, chunks, back_odd)
        return 0

    lax.fori_loop(0, MIDDLE + 7 + 2 * CUTS + chunks + 3 + chunks, step, 0)

    await_bytes(fac.at[:, 0], fac_sent)
    await_bytes(odd_v.at[:, :, pl.ds(0, 7)], odd_sent)
    await_bytes(even_f.at[0], even_sent)
    await_bytes(up_all.at[:, pl.ds(0, 3)], up_all_sent)
    await_bytes(up_own.at[:, pl.ds(0, 3)], up_own_sent)

    @pl.when(inner)
    def _():
        await_bytes(up_all, up_out_sent)

    @pl.when(jnp.logical_not(both(kind_b, child_here)))
    def _():
        await_bytes(up_all, up_first_sent)

    @pl.when(top)
    def _():
        await_bytes(up_all, full_sent.at[0])

    @pl.when(a_even)
    def _():
        await_bytes(up_all, full_sent.at[1])

    @pl.when(both(kind_a, jnp.logical_not(child_here)))
    def _():
        await_bytes(up_all, full_sent.at[2])

    @pl.when(odd)
    def _():
        await_bytes(mid.at[:, 0], mid_sent)
        await_bytes(base.at[:, pl.ds(0, 3)], base_sent)
        await_bytes(up_all, full_sent.at[3])
        await_bytes(own.at[:, pl.ds(0, 3)], own_sent)
        await_bytes(stage.at[0], out_kept)
        await_bytes(stage.at[0], out_sent)
        await_bytes(stage.at[0], out_sem)
        await_bytes(up_stage, up_stage_sent)

    @pl.when(both(odd, k == 0))
    def _():
        await_bytes(mid_out.at[pl.ds(0, CUTS)], mid_out_sent)

    @pl.when(both(odd, k == 1))
    def _():
        await_bytes(mid_out, mid_out_sent)

    @pl.when(even)
    def _():
        await_bytes(upp, upp_sent)
        await_bytes(upp.at[:, 0], upp_lent)
        await_bytes(shard, shard_sent)
        await_bytes(stage.at[0, 0], out_kept)
        await_bytes(stage.at[0, 0], out_sent)
        await_bytes(stage.at[0, 0], out_sem)
        await_bytes(up_stage.at[0], up_stage_kept)
        await_bytes(up_stage.at[0], up_stage_sent)
        await_bytes(up_stage.at[0], out_core_sem)
        await_bytes(up_stage, out_far_sem)


def local_solve(force, inverse, coupling):
    rhs, cols = force.shape[3:]
    block = inverse.shape[3]
    chunks = 2 * CUTS
    rows = 2 * rhs // CUTS
    wide = 2 * cols
    dma = pltpu.SemaphoreType.DMA
    piece = (rows, wide)
    panel = (chunks, CHIPS) + piece
    upper = (CUTS, CHIPS) + piece
    weight = (2, 2, block, cols)
    hbm = pl.BlockSpec(memory_space=pl.ANY)
    return pl.pallas_call(
        kernel,
        out_shape=jax.ShapeDtypeStruct(force.shape, F32),
        in_specs=[hbm] * 3,
        out_specs=hbm,
        scratch_shapes=[
            pltpu.VMEM((3, 2) + weight, BF16),
            pltpu.VMEM((3, 2) + weight, BF16),
            pltpu.VMEM((3,) + weight, BF16),
            pltpu.VMEM((2, 2, 2 * CHIPS, 2, rhs // 2, cols), BF16),
            pltpu.VMEM((2, 2, 2, rhs, cols), BF16),
            pltpu.VMEM(panel, BF16),
            pltpu.VMEM((CUTS,) + piece, BF16),
            pltpu.VMEM((chunks,) + piece, BF16),
            pltpu.VMEM((CUTS,) + piece, BF16),
            pltpu.VMEM((CUTS,) + piece, BF16),
            pltpu.VMEM(upper, BF16),
            pltpu.VMEM((3,) + upper, BF16),
            pltpu.VMEM((CUTS,) + piece, BF16),
            pltpu.VMEM(upper, BF16),
            pltpu.VMEM((CUTS,) + piece, F32),
            pltpu.VMEM(upper, BF16),
            pltpu.VMEM(upper, BF16),
            pltpu.VMEM((chunks,) + piece, F32),
            pltpu.VMEM((chunks,) + piece, F32),
            pltpu.VMEM(panel, BF16),
            pltpu.VMEM(panel, BF16),
            pltpu.VMEM((2, 2, 2, 2, rhs, cols), F32),
            pltpu.VMEM((2, 2, rhs, cols), F32),
            pltpu.VMEM((CHIPS,) + piece, F32),
            dma((3, 2)), dma((3, 2)), dma((3,)), dma((2, 2)), dma, dma((chunks,)), dma((CUTS,)), dma((CUTS,)),
            dma((CUTS,)), dma((3, CUTS)), dma((CUTS,)), dma((CUTS,)), dma((chunks,)), dma((chunks,)),
            dma, dma, dma,
            dma, dma, dma, dma, dma, dma, dma, dma, dma, dma, dma, dma, dma, dma((4,)), dma, dma, dma, dma, dma,
        ],
        compiler_params=pltpu.CompilerParams(
            collective_id=0, has_side_effects=True, vmem_limit_bytes=60 * 2**20
        ),
        name="resolvent",
    )(force, inverse, coupling)


def solution(mesh):
    return jax.shard_map(
        local_solve,
        mesh=mesh,
        in_specs=(
            P(None, "radial", None, None, "col"),
            P(None, "radial", None, None, "col"),
            P(None, "radial", None, None, None, "col"),
        ),
        out_specs=P(None, "radial", None, None, "col"),
        check_vma=False,
    )
```

time: 146 us -> 121 us (0.83)
  Pallas kernels: 141 us -> 118 us
  local copies, waits for them, and re-layouts: 4.2 us -> 2.3 us
    pallas_call x1, Pallas kernels: 141 us -> 118 us  [local_solve(): pl.pallas_call(kernel, out_shape=jax.ShapeDtypeStruct(force.shape, F32),...]
    unnamed x5 -> x1, local copies, waits for them, and re-layouts: 4.2 us -> 2.3 us
where the time goes in v2:
time: 121 us; the launch traced here: 120 us
  Pallas kernels  118 us (98%)
  local copies, waits for them, and re-layouts  2.3 us (2%)
    pallas_call x1, Pallas kernels, local_solve(): pl.pallas_call(kernel, out_shape=jax.ShapeDtypeStruct(force.shape, F32),...  118 us

profile of v2, /device:TPU:27, one launch (start us, length us, event | category | flops | bytes accessed | tf_op | source)
XLA Modules:
  0.0 120.1 jit_solution(3183913758835474844)
XLA Ops:
  0.0 117.8 %resolvent.1 = f32[4,2,2,128,128]{4,3,2,1,0:T(8,128)} custom-call(bf16[4,2,2,128,128]{4,3,2,1,0:T(8,128)(2,1)} %force.1, bf16[4,2,2,1024,128]{4,3,2,1,0:T(8,128)(2,1)} %inverse.1, bf16[4,2,2,2,1024,128]{5,4,3,2,1,0:T(8,128)(2,1)} %coupling.1), custom_call_target="tpu_custom_call" | custom-call | tf_op jit(solution)/shard_map/resolvent/pallas_call | solution.py:553
  117.8 2.3 %copy.5 = f32[4,2,2,128,128]{4,3,2,1,0:T(8,128)} copy(f32[4,2,2,128,128]{4,3,2,1,0:T(8,128)} %resolvent.1) | data formatting | bytes 2097152

commit v3 on v2

--- a/solution.py
+++ b/solution.py
@@ -13,6 +13,7 @@
 C0, INV, C1 = range(3)
 MIDDLE = 3
 SETTLE = 2
+PIECES = 8
 
 
 def kernel(
@@ -20,9 +21,9 @@
     fac, mid, upp, odd_v, even_f, base, shard, mid_out, up_base, up_mid, up_all, up_upd, up_out, up_red,
     up_inv, up_low, up_own, inv_even, inv_odd, low, own, stage, up_stage, acc,
     fac_sem, mid_sem, upp_sem, odd_sem, even_sem, base_sem, up_base_sem, up_mid_sem, up_all_sem, up_upd_sem,
-    up_low_sem, up_own_sem, low_sem, own_sem, out_sem, out_core_sem, out_far_sem,
+    up_low_sem, low_sem, own_sem, up_shard_sem, low_shard_sem, own_shard_sem, out_sem, out_core_sem, out_far_sem,
     fac_sent, mid_sent, upp_lent, upp_sent, odd_sent, even_sent, base_sent, shard_sent, mid_out_sent,
-    up_all_sent, up_out_sent, up_first_sent, up_own_sent, full_sent, own_sent, out_sent, out_kept,
+    up_all_sent, up_out_sent, up_first_sent, shard_out_sent, up_low_sent, low_sent, own_sent, out_sent, out_kept,
     up_stage_sent, up_stage_kept,
 ):
     chunks = base.shape[0]
@@ -49,6 +50,7 @@
     beside = 4 * x + lax.rem(y + 1 + 2 * k, 4)
     child = 4 * x + jnp.where(kind_a, 1, 3)
     child_here = child == p
+    by_shard = jnp.logical_or(jnp.logical_and(height == 1, x == 1), jnp.logical_and(kind_b, lax.rem(x, 2) == 0))
 
     def both(one, two):
         return jnp.logical_and(one, two)
@@ -96,7 +98,7 @@
         def _():
             keep(which, 0, mid, mid_sem)
 
-        @pl.when(even)
+        @pl.when(even if which == INV else both(even, p > 0))
         def _():
             local(factor(which, 0, 2 * k), upp.at[which, k], upp_sem.at[which])
 
@@ -161,18 +163,25 @@
                         send()
                     else:
                         pl.when(core != k)(send)
+    def spread_factor(which, n=0, of=1):
+        size = coupling.shape[4] // of
+        at = pl.ds(pl.multiple_of(n * size, size), size)
+        for core in range(2):
+            remote(
+                factor(which, 0, 2 * core + 1).at[:, at], upp.at[which, k, :, at], upp_sent, upp_sem.at[which],
+                4 * x + lax.rem(y + 1 + 2 * core, 4), 2 * z + core,
+            )
+
+    pl.when(p == 0)(lambda: spread_factor(INV))
+    pl.when(both(even, p > 0))(lambda: spread_factor(C0))
+
     for which in (C0, INV, C1):
         @pl.when(odd)
         def _():
             lend(which, 0, mid, mid_sem, mid_sent)
 
-        @pl.when(even)
-        def _():
-            for core in range(2):
-                remote(
-                    factor(which, 0, 2 * core + 1), upp.at[which, k], upp_sent, upp_sem.at[which],
-                    4 * x + lax.rem(y + 1 + 2 * core, 4), 2 * z + core,
-                )
+        @pl.when(even if which == INV else both(even, p > 0))
+        def _():
             remote(
                 factor(which, 0, 2 * other), upp.at[which, k], upp_lent, upp_sem.at[which],
                 p, 2 * z + other,
@@ -332,15 +341,8 @@
         along(up_all, j, up_all_sent, up_all_sem)
 
     def reduce_upper(j):
-        @pl.when(j == 0)
-        def _():
-            await_upper(C0)
-
-            @pl.when(top)
-            def _():
-                await_upper(INV)
-                await_upper(C1)
-
+        once(j, lambda: pl.when(inner)(lambda: await_upper(C0)))
+        once(j, lambda: pl.when(top)(lambda: await_upper(INV)))
         await_bytes(up_all.at[j, pl.ds(0, 3)], up_all_sem.at[j])
 
         @pl.when(height == 0)
@@ -374,82 +376,103 @@
         up_inv[j] = times(across(up_red, j), upp.at[INV])
 
     def solved_upper(j, value):
-        up_own[j, z] = value.astype(BF16)
+        i = up_g * CUTS + j
+        panel = value.astype(BF16)
+        up_own[j] = panel
 
         @pl.when(height > 0)
         def _():
-            straight(up_own.at[j, z], up_low.at[j, z], up_first_sent, up_low_sem.at[j], first)
+            straight(up_own.at[j], up_low.at[j, z], up_first_sent, up_low_sem.at[j], first)
 
         @pl.when(both(kind_b, jnp.logical_not(child_here)))
         def _():
-            i = up_g * CUTS + j
-            straight(up_own.at[j, z], low.at[i, z], up_first_sent, low_sem.at[i], child)
-
-        along(up_own, j, up_own_sent, up_own_sem)
+            straight(up_own.at[j], low.at[i, z], up_first_sent, low_sem.at[i], child)
+
+        @pl.when(child_here)
+        def _():
+            low[i, z] = panel
+            along(low, i, low_sent, low_sem)
+
+        @pl.when(top)
+        def _():
+            remote(up_own.at[j], up_low.at[j, z], shard_out_sent.at[0], up_shard_sem.at[j], p + 4, c)
+
+        @pl.when(a_even)
+        def _():
+            remote(up_own.at[j], up_low.at[j, z], shard_out_sent.at[1], up_shard_sem.at[j], twin, c)
+
+        @pl.when(both(kind_a, jnp.logical_not(child_here)))
+        def _():
+            remote(up_own.at[j], low.at[i, z], shard_out_sent.at[2], low_shard_sem.at[i], child, c)
+
+        @pl.when(odd)
+        def _():
+            remote(up_own.at[j], own.at[i, z], shard_out_sent.at[3], own_shard_sem.at[j], home, c)
+
+        @pl.when(even)
+        def _():
+            own[i, z] = panel
+            along(own, i, own_sent, own_sem)
+
         write_upper(j, value)
 
-    def pass_upper(j):
-        i = up_g * CUTS + j
-        await_bytes(up_own.at[j, pl.ds(0, 3)], up_own_sem.at[j])
-
-        @pl.when(child_here)
-        def _():
-            local(up_own.at[j], low.at[i], low_sem.at[i])
-
-        @pl.when(top)
-        def _():
-            remote(up_own.at[j], up_low.at[j], full_sent.at[0], up_low_sem.at[j], p + 4, c)
-
-        @pl.when(a_even)
-        def _():
-            remote(up_own.at[j], up_low.at[j], full_sent.at[1], up_low_sem.at[j], twin, c)
-
-        @pl.when(both(kind_a, jnp.logical_not(child_here)))
-        def _():
-            remote(up_own.at[j], low.at[i], full_sent.at[2], low_sem.at[i], child, c)
-
-        @pl.when(odd)
-        def _():
-            remote(up_own.at[j], own.at[i], full_sent.at[3], own_sem.at[i], home, c)
+    def spread_upper(j):
+        await_bytes(up_low.at[j, 0], up_shard_sem.at[j])
+        along(up_low, j, up_low_sent, up_low_sem)
+
+    def spread_low(i):
+        @pl.when(jnp.logical_not(both(child_here, i >= CUTS)))
+        def _():
+            await_bytes(low.at[i, 0], low_shard_sem.at[i])
+            along(low, i, low_sent, low_sem)
+
+    def spread_own(j):
+        await_bytes(own.at[CUTS + j, 0], own_shard_sem.at[j])
+        along(own, CUTS + j, own_sent, own_sem)
 
     def back_upper(j):
         once(j, lambda: await_upper(C1))
-        await_bytes(up_low.at[j], up_low_sem.at[j])
+
+        @pl.when(by_shard)
+        def _():
+            await_bytes(up_low.at[j, pl.ds(0, 3)], up_low_sem.at[j])
+
+        @pl.when(jnp.logical_not(by_shard))
+        def _():
+            await_bytes(up_low.at[j], up_low_sem.at[j])
+
         solved_upper(j, up_inv[j] - times(across(up_low, j), upp.at[C1]))
 
     def back_middle(i):
         g, _, _, _ = place(i)
         once(i, lambda: await_factor(mid, C1, mid_sem))
-        await_bytes(low.at[i], low_sem.at[i])
+        whole = both(y == 3, jnp.logical_not(both(child_here, g == 1)))
+
+        @pl.when(whole)
+        def _():
+            await_bytes(low.at[i], low_sem.at[i])
+
+        @pl.when(jnp.logical_not(whole))
+        def _():
+            await_bytes(low.at[i, pl.ds(0, 3)], low_sem.at[i])
+
         value = inv_even[i] - times(across(low, i), mid.at[C1, g])
         own[i, z] = value.astype(BF16)
         along(own, i, own_sent, own_sem)
         write_out(i, 0, value)
 
     def back_odd(i):
-        g, q, _, _ = place(i)
+        g, _, _, _ = place(i)
         once(i, lambda: await_factor(fac, C1, fac_sem))
 
-        @pl.when(odd)
-        def _():
-            await_bytes(own.at[i, pl.ds(0, 3)], own_sem.at[i])
-
-        @pl.when(both(even, g == 0))
-        def _():
-            own[i] = up_own[q]
-
-        @pl.when(both(even, g == 1))
-        def _():
-            await_bytes(own.at[i], own_sem.at[i])
-
+        await_bytes(own.at[i, pl.ds(0, 3)], own_sem.at[i])
         write_out(i, 1, inv_odd[i] - times(across(own, i), fac.at[C1, g]))
 
     at_settle = jnp.where(even, MIDDLE + 3, MIDDLE + 7)
     at_upper = at_settle + jnp.where(kind_b, SETTLE, CUTS)
     at_middle_inverse = MIDDLE + 7 + 2 * CUTS
-    at_back = at_middle_inverse + chunks
-    at_pass = jnp.where(top, at_upper, at_back) + SETTLE
-    at_end = at_back + 3
+    at_back = at_middle_inverse + chunks + CUTS
+    at_end = at_back + SETTLE + 3
 
     for g in range(2):
         await_bytes(fac.at[C0, g], fac_sem.at[C0, g])
@@ -465,25 +488,29 @@
                 work(i)
 
         during(0, chunks, reduce_odd)
+        during(CUTS, PIECES, lambda n: spread_factor(INV, n, PIECES), both(even, p > 0))
+        during(CUTS + PIECES, PIECES, lambda n: spread_factor(C1, n, PIECES), both(even, p > 0))
         during(MIDDLE, chunks, reduce_middle, odd)
         during(MIDDLE + 1, chunks, inverse_odd)
         during(at_settle, CUTS, settle_upper)
         during(at_upper, CUTS, reduce_upper)
-        during(at_upper, CUTS, inverse_upper, inner)
+        during(jnp.where(even, at_upper, at_back - CUTS), CUTS, inverse_upper, inner)
         during(at_middle_inverse, chunks, inverse_middle, odd)
-        during(at_back, CUTS, back_upper, inner)
-        during(at_pass, CUTS, pass_upper)
-        during(at_back, chunks, back_middle, odd)
+        during(at_back, CUTS, spread_upper, by_shard)
+        during(at_back + SETTLE, CUTS, back_upper, inner)
+        during(at_back, chunks, spread_low, y == 1)
+        during(at_back + SETTLE, chunks, back_middle, odd)
+        during(at_back + SETTLE + CUTS, CUTS, spread_own, even)
         during(at_end, chunks, back_odd)
         return 0
 
-    lax.fori_loop(0, MIDDLE + 7 + 2 * CUTS + chunks + 3 + chunks, step, 0)
+    lax.fori_loop(0, at_end + chunks, step, 0)
 
     await_bytes(fac.at[:, 0], fac_sent)
     await_bytes(odd_v.at[:, :, pl.ds(0, 7)], odd_sent)
     await_bytes(even_f.at[0], even_sent)
     await_bytes(up_all.at[:, pl.ds(0, 3)], up_all_sent)
-    await_bytes(up_own.at[:, pl.ds(0, 3)], up_own_sent)
+    await_bytes(own.at[:, pl.ds(0, 3)], own_sent)
 
     @pl.when(inner)
     def _():
@@ -495,27 +522,38 @@
 
     @pl.when(top)
     def _():
-        await_bytes(up_all, full_sent.at[0])
+        await_bytes(up_own, shard_out_sent.at[0])
 
     @pl.when(a_even)
     def _():
-        await_bytes(up_all, full_sent.at[1])
+        await_bytes(up_own, shard_out_sent.at[1])
 
     @pl.when(both(kind_a, jnp.logical_not(child_here)))
     def _():
-        await_bytes(up_all, full_sent.at[2])
+        await_bytes(up_own, shard_out_sent.at[2])
 
     @pl.when(odd)
     def _():
         await_bytes(mid.at[:, 0], mid_sent)
         await_bytes(base.at[:, pl.ds(0, 3)], base_sent)
-        await_bytes(up_all, full_sent.at[3])
-        await_bytes(own.at[:, pl.ds(0, 3)], own_sent)
+        await_bytes(up_own, shard_out_sent.at[3])
         await_bytes(stage.at[0], out_kept)
         await_bytes(stage.at[0], out_sent)
         await_bytes(stage.at[0], out_sem)
         await_bytes(up_stage, up_stage_sent)
 
+    @pl.when(by_shard)
+    def _():
+        await_bytes(up_low.at[:, pl.ds(0, 3)], up_low_sent)
+
+    @pl.when(y == 1)
+    def _():
+        await_bytes(low.at[:, pl.ds(0, 3)], low_sent)
+
+    @pl.when(both(y == 3, k == 0))
+    def _():
+        await_bytes(low.at[pl.ds(0, CUTS), pl.ds(0, 3)], low_sent)
+
     @pl.when(both(odd, k == 0))
     def _():
         await_bytes(mid_out.at[pl.ds(0, CUTS)], mid_out_sent)
@@ -524,10 +562,18 @@
     def _():
         await_bytes(mid_out, mid_out_sent)
 
-    @pl.when(even)
+    @pl.when(p == 0)
+    def _():
+        await_bytes(upp.at[INV], upp_sent)
+        await_bytes(upp.at[INV, 0], upp_lent)
+
+    @pl.when(both(even, p > 0))
     def _():
         await_bytes(upp, upp_sent)
         await_bytes(upp.at[:, 0], upp_lent)
+
+    @pl.when(even)
+    def _():
         await_bytes(shard, shard_sent)
         await_bytes(stage.at[0, 0], out_kept)
         await_bytes(stage.at[0, 0], out_sent)
@@ -572,7 +618,7 @@
             pltpu.VMEM(upper, BF16),
             pltpu.VMEM((CUTS,) + piece, F32),
             pltpu.VMEM(upper, BF16),
-            pltpu.VMEM(upper, BF16),
+            pltpu.VMEM((CUTS,) + piece, BF16),
             pltpu.VMEM((chunks,) + piece, F32),
             pltpu.VMEM((chunks,) + piece, F32),
             pltpu.VMEM(panel, BF16),
@@ -581,9 +627,9 @@
             pltpu.VMEM((2, 2, rhs, cols), F32),
             pltpu.VMEM((CHIPS,) + piece, F32),
             dma((3, 2)), dma((3, 2)), dma((3,)), dma((2, 2)), dma, dma((chunks,)), dma((CUTS,)), dma((CUTS,)),
-            dma((CUTS,)), dma((3, CUTS)), dma((CUTS,)), dma((CUTS,)), dma((chunks,)), dma((chunks,)),
-            dma, dma, dma,
-            dma, dma, dma, dma, dma, dma, dma, dma, dma, dma, dma, dma, dma, dma((4,)), dma, dma, dma, dma, dma,
+            dma((CUTS,)), dma((3, CUTS)), dma((CUTS,)), dma((chunks,)), dma((chunks,)), dma((CUTS,)),
+            dma((chunks,)), dma((CUTS,)), dma, dma, dma,
+            dma, dma, dma, dma, dma, dma, dma, dma, dma, dma, dma, dma, dma((4,)), dma, dma, dma, dma, dma, dma, dma,
         ],
         compiler_params=pltpu.CompilerParams(
             collective_id=0, has_side_effects=True, vmem_limit_bytes=60 * 2**20

time: 121 us -> 105 us (0.87)
  Pallas kernels: 118 us -> 102 us
    pallas_call x1, Pallas kernels: 118 us -> 102 us  [local_solve(): pl.pallas_call(kernel, out_shape=jax.ShapeDtypeStruct(force.shape, F32),...]
where the time goes in v3:
time: 105 us
  Pallas kernels  102 us (97%)
  local copies, waits for them, and re-layouts  2.3 us (2%)
    pallas_call x1, Pallas kernels, local_solve(): pl.pallas_call(kernel, out_shape=jax.ShapeDtypeStruct(force.shape, F32),...  102 us
    unnamed x1, local copies, waits for them, and re-layouts  2.3 us

profile of v3, /device:TPU:27, one launch (start us, length us, event | category | flops | bytes accessed | tf_op | source)
XLA Modules:
  0.0 104.7 jit_solution(7460694975619517229)
XLA Ops:
  0.0 102.3 %resolvent.1 = f32[4,2,2,128,128]{4,3,2,1,0:T(8,128)} custom-call(bf16[4,2,2,128,128]{4,3,2,1,0:T(8,128)(2,1)} %force.1, bf16[4,2,2,1024,128]{4,3,2,1,0:T(8,128)(2,1)} %inverse.1, bf16[4,2,2,2,1024,128]{5,4,3,2,1,0:T(8,128)(2,1)} %coupling.1), custom_call_target="tpu_custom_call" | custom-call | tf_op jit(solution)/shard_map/resolvent/pallas_call | solution.py:599
  102.4 2.3 %copy.5 = f32[4,2,2,128,128]{4,3,2,1,0:T(8,128)} copy(f32[4,2,2,128,128]{4,3,2,1,0:T(8,128)} %resolvent.1) | data formatting | bytes 2097152

commit v4 on v3

--- a/solution.py
+++ b/solution.py
@@ -13,6 +13,9 @@
 C0, INV, C1 = range(3)
 MIDDLE = 3
 SETTLE = 2
+AHEAD = 4
+PIECE_CORE = [0, 0, 1, 0, 1, 0, 1, 1]
+PIECE_OF_CORE = [0, 1, 0, 2, 1, 3, 2, 3]
 PIECES = 8
 
 
@@ -150,19 +153,34 @@
 
     lend(C0, 1, fac, fac_sem, fac_sent)
     remote(force.at[pl.ds(2 * other, 2), 0], even_f.at[k], even_sent, even_sem, p, 2 * z + other)
-    for g in range(2):
-        for h in range(2):
-            for step in (1, 3, 2, 0):
-                for core in range(2):
-                    def send():
-                        remote(
-                            force.at[2 * core + g, 1, :, pl.ds(h * half, half)],
-                            odd_v.at[g, h, c], odd_sent, odd_sem.at[g, h], p, 2 * ring(step) + core,
-                        )
-                    if step:
-                        send()
-                    else:
-                        pl.when(core != k)(send)
+    def pick(n, values):
+        found = values[-1]
+        for at in range(len(values) - 1):
+            found = jnp.where(n == at, values[at], found)
+        return found
+
+    def send_odd(n, _):
+        core, piece = pick(n, PIECE_CORE), pick(n, PIECE_OF_CORE)
+        g, h = lax.div(piece, 2), lax.rem(piece, 2)
+        src = force.at[2 * core + g, 1, :, pl.ds(pl.multiple_of(h * half, half), half)]
+        for step in (2, 1, 3):
+            remote(src, odd_v.at[g, h, c], odd_sent, odd_sem.at[g, h], p, 2 * ring(step) + core)
+
+        @pl.when(core != k)
+        def _():
+            remote(src, odd_v.at[g, h, c], odd_sent, odd_sem.at[g, h], p, 2 * z + core)
+
+        return 0
+
+    def allowed(piece):
+        come = jnp.where(
+            k == 0, pick(piece, [n for n in range(8) if PIECE_CORE[n] == 0]),
+            pick(piece, [n for n in range(8) if PIECE_CORE[n] == 1]),
+        )
+        return jnp.minimum(come + 1 + AHEAD, 8)
+
+    lax.fori_loop(0, AHEAD, send_odd, 0)
+
     def spread_factor(which, n=0, of=1):
         size = coupling.shape[4] // of
         at = pl.ds(pl.multiple_of(n * size, size), size)
@@ -224,8 +242,8 @@
             remote(ref.at[i, z], ref.at[i, z], sent, sem.at[i], p, 2 * ring(step) + k)
 
     def straight(src, dst, sent, got, column):
-        for chip in range(CHIPS):
-            remote(src, dst, sent, got, column, 2 * chip + k)
+        for step in (2, 1, 3, 0):
+            remote(src, dst, sent, got, column, 2 * ring(step) + k)
 
     def write_out(i, row, value):
         g, q, _, _ = place(i)
@@ -278,6 +296,9 @@
         @pl.when(lax.rem(q, CUTS // 2) == 0)
         def _():
             await_bytes(odd_v.at[g, h], odd_sem.at[g, h])
+            piece = 2 * g + h
+            sent = jnp.where(piece == 0, AHEAD, allowed(piece - 1))
+            lax.fori_loop(sent, jnp.where(piece == 3, 8, allowed(piece)), send_odd, 0)
 
         at = rows_of(q)
         mine = jnp.concatenate(
@@ -488,8 +509,9 @@
                 work(i)
 
         during(0, chunks, reduce_odd)
-        during(CUTS, PIECES, lambda n: spread_factor(INV, n, PIECES), both(even, p > 0))
-        during(CUTS + PIECES, PIECES, lambda n: spread_factor(C1, n, PIECES), both(even, p > 0))
+        at_move = jnp.where(kind_a, CUTS, MIDDLE + 3 + SETTLE + CUTS)
+        during(at_move, PIECES, lambda n: spread_factor(INV, n, PIECES), both(even, p > 0))
+        during(at_move + PIECES, PIECES, lambda n: spread_factor(C1, n, PIECES), both(even, p > 0))
         during(MIDDLE, chunks, reduce_middle, odd)
         during(MIDDLE + 1, chunks, inverse_odd)
         during(at_settle, CUTS, settle_upper)

time: 105 us -> 98.9 us (0.942)
  Pallas kernels: 102 us -> 95.9 us
    pallas_call x1, Pallas kernels: 102 us -> 95.9 us  [local_solve(): pl.pallas_call(kernel, out_shape=jax.ShapeDtypeStruct(force.shape, F32),...]
where the time goes in v4:
time: 98.9 us; the launch traced here: 98.2 us
  Pallas kernels  95.9 us (97%)
  local copies, waits for them, and re-layouts  2.3 us (2%)
    pallas_call x1, Pallas kernels, local_solve(): pl.pallas_call(kernel, out_shape=jax.ShapeDtypeStruct(force.shape, F32),...  95.9 us
    unnamed x1, local copies, waits for them, and re-layouts  2.3 us

profile of v4, /device:TPU:27, one launch (start us, length us, event | category | flops | bytes accessed | tf_op | source)
XLA Modules:
  0.0 98.2 jit_solution(5058912229343912783)
XLA Ops:
  0.0 95.9 %resolvent.1 = f32[4,2,2,128,128]{4,3,2,1,0:T(8,128)} custom-call(bf16[4,2,2,128,128]{4,3,2,1,0:T(8,128)(2,1)} %force.1, bf16[4,2,2,1024,128]{4,3,2,1,0:T(8,128)(2,1)} %inverse.1, bf16[4,2,2,2,1024,128]{5,4,3,2,1,0:T(8,128)(2,1)} %coupling.1), custom_call_target="tpu_custom_call" | custom-call | tf_op jit(solution)/shard_map/resolvent/pallas_call | solution.py:621
  95.9 2.3 %copy.5 = f32[4,2,2,128,128]{4,3,2,1,0:T(8,128)} copy(f32[4,2,2,128,128]{4,3,2,1,0:T(8,128)} %resolvent.1) | data formatting | bytes 2097152

commit v5 on v4

--- a/solution.py
+++ b/solution.py
@@ -251,11 +251,20 @@
         for side in range(2):
             for part in range(2):
                 stage[side, g, row, part, at] = value[part * cut:(part + 1) * cut, side * 128:(side + 1) * 128]
-        local(stage.at[k, g, row, :, at], out.at[2 * k + g, row, :, at], out_kept)
-        remote(
-            stage.at[other, g, row, :, at], out.at[2 * k + g, row, :, at], out_sent, out_sem,
-            p, 2 * z + other,
-        )
+        if row:
+            local(stage.at[k, g, row, :, at], out.at[2 * k + g, row, :, at], out_kept)
+            remote(
+                stage.at[other, g, row, :, at], out.at[2 * k + g, row, :, at], out_sent, out_sem,
+                p, 2 * z + other,
+            )
+            return
+
+        @pl.when(q == CUTS - 1)
+        def _():
+            local(stage.at[k, g, row], out.at[2 * k + g, row], out_kept)
+            remote(
+                stage.at[other, g, row], out.at[2 * k + g, row], out_sent, out_sem, p, 2 * z + other
+            )
 
     def write_upper(j, value):
         at = rows_of(j)
@@ -264,20 +273,16 @@
             for part in range(2):
                 up_stage[side, part, at] = value[part * cut:(part + 1) * cut, side * 128:(side + 1) * 128]
 
-        @pl.when(even)
-        def _():
-            local(up_stage.at[k, :, at], out.at[freq, 0, :, at], up_stage_kept)
-            remote(
-                up_stage.at[other, :, at], out.at[freq, 0, :, at], up_stage_sent, out_core_sem,
-                p, 2 * z + other,
-            )
-
-        @pl.when(odd)
+        @pl.when(both(even, j == CUTS - 1))
+        def _():
+            local(up_stage.at[k], out.at[freq, 0], up_stage_kept)
+            remote(up_stage.at[other], out.at[freq, 0], up_stage_sent, out_core_sem, p, 2 * z + other)
+
+        @pl.when(both(odd, j == CUTS - 1))
         def _():
             for side in range(2):
                 remote(
-                    up_stage.at[side, :, at], out.at[freq, 0, :, at], up_stage_sent, out_far_sem,
-                    home, 2 * z + side,
+                    up_stage.at[side], out.at[freq, 0], up_stage_sent, out_far_sem, home, 2 * z + side
                 )
 
     def await_factor(ref, which, sem):
@@ -511,7 +516,7 @@
         during(0, chunks, reduce_odd)
         at_move = jnp.where(kind_a, CUTS, MIDDLE + 3 + SETTLE + CUTS)
         during(at_move, PIECES, lambda n: spread_factor(INV, n, PIECES), both(even, p > 0))
-        during(at_move + PIECES, PIECES, lambda n: spread_factor(C1, n, PIECES), both(even, p > 0))
+        during(at_move + jnp.where(kind_a, 2, PIECES), PIECES, lambda n: spread_factor(C1, n, PIECES), both(even, p > 0))
         during(MIDDLE, chunks, reduce_middle, odd)
         during(MIDDLE + 1, chunks, inverse_odd)
         during(at_settle, CUTS, settle_upper)

time: 98.9 us -> 98.5 us (level)
  no operation moved by 1% of the time
where the time goes in v5:
time: 98.5 us; the launch traced here: 98.4 us
  Pallas kernels  96 us (97%)
  local copies, waits for them, and re-layouts  2.3 us (2%)
    pallas_call x1, Pallas kernels, local_solve(): pl.pallas_call(kernel, out_shape=jax.ShapeDtypeStruct(force.shape, F32),...  96 us
    unnamed x1, local copies, waits for them, and re-layouts  2.3 us

profile of v5, /device:TPU:27, one launch (start us, length us, event | category | flops | bytes accessed | tf_op | source)
XLA Modules:
  0.0 98.4 jit_solution(8796111721921629895)
XLA Ops:
  0.0 96.0 %resolvent.1 = f32[4,2,2,128,128]{4,3,2,1,0:T(8,128)} custom-call(bf16[4,2,2,128,128]{4,3,2,1,0:T(8,128)(2,1)} %force.1, bf16[4,2,2,1024,128]{4,3,2,1,0:T(8,128)(2,1)} %inverse.1, bf16[4,2,2,2,1024,128]{5,4,3,2,1,0:T(8,128)(2,1)} %coupling.1), custom_call_target="tpu_custom_call" | custom-call | tf_op jit(solution)/shard_map/resolvent/pallas_call | solution.py:626
  96.1 2.3 %copy.5 = f32[4,2,2,128,128]{4,3,2,1,0:T(8,128)} copy(f32[4,2,2,128,128]{4,3,2,1,0:T(8,128)} %resolvent.1) | data formatting | bytes 2097152
